TPU v7x, 32 devices: a whole 2x2x4 slice. The times are simulated.
32 devices in a mesh: tm: 8 (over y, x, core), height: 4 (over z).
Axes of the slice: x: 2, y: 2, z: 4, core: 2. Of those that a mesh axis runs over, the one named last changes fastest.
Arguments:
- query_band: bfloat16 [24, 24, 24, 2048], P('tm', 'height'), may hold values from -4.5 to 4.5
- key_band: bfloat16 [24, 24, 24, 2048], P('tm', 'height'), may hold values from -11 to 11
- value_band: bfloat16 [24, 24, 24, 2048], P('tm', 'height'), may hold values from -6 to 6
Outputs:
- attended: bfloat16 [24, 24, 24, 2048], P('tm', 'height')
All inputs are finite; a program needn't handle non-finite values.
Results may differ from a plain program's by a relative error of at most 0.0033.
Values may be sent and summed in bfloat16 or wider, within the bound.
A program may use at most 128 MiB of HBM per device.

v0:
```python
import jax
import jax.numpy as jnp
from jax import lax
from jax.sharding import PartitionSpec as P

HEAD_DIM = 128
TILE_T = 6
TILE_H = 8
TILE_W = 8


def from_behind(value, axis, steps):
    count = lax.axis_size(axis)
    leading, last = (max(0, -steps), min(count, count - steps))
    return lax.ppermute(value, axis, [(source, source + steps) for source in range(leading, last)])


def attend_plane(queries, window, time_ok):
    part_frames, rows_all, cols_all, local_features = queries.shape
    local_heads = local_features // HEAD_DIM
    window_frames = window.shape[1]
    key_count = window_frames * rows_all * cols_all
    head_window = jnp.transpose(window.reshape(2, key_count, local_heads, HEAD_DIM), (0, 2, 1, 3))
    key_rows = head_window[0]
    value_rows = head_window[1]
    head_queries = jnp.transpose(
        queries.reshape(part_frames, rows_all, cols_all, local_heads, HEAD_DIM), (3, 0, 1, 2, 4)
    )
    frame_tile = jnp.arange(window_frames, dtype=jnp.int32) // TILE_T
    row_tile = jnp.arange(rows_all, dtype=jnp.int32) // TILE_H
    col_tile = jnp.arange(cols_all, dtype=jnp.int32) // TILE_W
    grid_shape = (window_frames, rows_all, cols_all)
    key_time = jnp.broadcast_to(time_ok[frame_tile][:, None, None], grid_shape).reshape(-1)
    key_row = jnp.broadcast_to(row_tile[None, :, None], grid_shape).reshape(-1)
    key_col = jnp.broadcast_to(col_tile[None, None, :], grid_shape).reshape(-1)
    row_count = rows_all // TILE_H
    col_count = cols_all // TILE_W
    zero_index = jnp.zeros((), jnp.int32)
    query_count = part_frames * TILE_H * TILE_W

    def one_tile(tile_id):
        row_index = tile_id // col_count
        col_index = tile_id % col_count
        query_block = lax.dynamic_slice(
            head_queries,
            (zero_index, zero_index, row_index * TILE_H, col_index * TILE_W, zero_index),
            (local_heads, part_frames, TILE_H, TILE_W, HEAD_DIM),
        ).reshape(local_heads, query_count, HEAD_DIM)
        usable = (
            key_time & (jnp.abs(key_row - row_index) <= 1) & (jnp.abs(key_col - col_index) <= 1)
        )
        scores = jnp.einsum(
            "hqd,hkd->hqk", query_block, key_rows, preferred_element_type=jnp.float32
        ) * HEAD_DIM ** (-0.5)
        scores = jnp.where(usable[None, None, :], scores, jnp.float32(-1e30))
        largest = jnp.max(scores, axis=2, keepdims=True)
        weights = lax.optimization_barrier(jnp.exp(scores - largest).astype(jnp.bfloat16))
        weight_sum = jnp.sum(weights.astype(jnp.float32), axis=2, keepdims=True)
        summed = jnp.einsum("hqk,hkd->hqd", weights, value_rows, preferred_element_type=jnp.float32)
        return (summed / weight_sum).astype(jnp.bfloat16)

    tile_outputs = lax.map(one_tile, jnp.arange(row_count * col_count, dtype=jnp.int32))
    tile_outputs = tile_outputs.reshape(
        row_count, col_count, local_heads, part_frames, TILE_H, TILE_W, HEAD_DIM
    )
    return jnp.transpose(tile_outputs, (3, 0, 4, 1, 5, 2, 6)).reshape(
        part_frames, rows_all, cols_all, local_features
    )


def body(query_band, key_band, value_band):
    parity = lax.axis_index("tm") % 2
    relaid = (
        lax.all_to_all(query_band, "height", split_axis=3, concat_axis=1, tiled=True),
        lax.all_to_all(key_band, "height", split_axis=3, concat_axis=1, tiled=True),
        lax.all_to_all(value_band, "height", split_axis=3, concat_axis=1, tiled=True),
    )
    queries = relaid[0]
    pair_local = jnp.stack([relaid[1], relaid[2]])
    part_frames = pair_local.shape[1]
    pieces = []
    for step_by in (3, 2, 1, 0, -1, -2, -3):
        if step_by == 0:
            pieces.append(pair_local)
        else:
            pieces.append(from_behind(pair_local, "tm", step_by))
    spread = jnp.concatenate(pieces, axis=1)
    window = lax.dynamic_slice_in_dim(spread, (1 - parity) * part_frames, 3 * TILE_T, 1)
    time_index = lax.axis_index("tm") // 2
    time_tiles = lax.axis_size("tm") // 2
    offsets = jnp.arange(3, dtype=jnp.int32) - 1
    time_ok = (time_index + offsets >= 0) & (time_index + offsets < time_tiles)
    attended_heads = attend_plane(queries, window, time_ok)
    return lax.all_to_all(attended_heads, "height", split_axis=1, concat_axis=3, tiled=True)


def solution(mesh):
    return jax.shard_map(
        body,
        mesh=mesh,
        in_specs=(
            P("tm", "height", None, None),
            P("tm", "height", None, None),
            P("tm", "height", None, None),
        ),
        out_specs=P("tm", "height", None, None),
        check_vma=False,
    )
```

profile of v0, /device:TPU:2, one launch (start us, length us, event | category | flops | bytes accessed | tf_op | source)
XLA Modules:
  0.0 1067.3 jit_solution(12677338735186013389)
XLA Ops:
  13.1 15.3 %reshape.175 = bf16[4,2,110592]{2,1,0:T(2,128)(2,1)} reshape(bf16[2048,3,6,24]{3,2,1,0:T(8,128)(2,1)} %bitcast.70) | data formatting | bytes 3538944
  44.7 15.2 %reshape.173 = bf16[4,2,110592]{2,1,0:T(2,128)(2,1)} reshape(bf16[2048,3,6,24]{3,2,1,0:T(8,128)(2,1)} %bitcast.71) | data formatting | bytes 3538944
  59.8 14.6 %all-to-all-done.1 = bf16[4,2,110592]{2,1,0:T(2,128)(2,1)S(1)} async-done(((bf16[4,2,110592]{2,1,0:T(2,128)(2,1)}), bf16[4,2,110592]{2,1,0:T(2,128)(2,1)S(1)}, u32[]{:S(2)}, u32[]{:S(2)}) %all-to-all-start.1) | async-done | bytes 1769504 | tf_op jit(solution)/shard_map/all_to_all | solution.py:75
  78.2 16.1 %reshape.176 = bf16[2048,3,6,24]{3,2,1,0:T(8,128)(2,1)} reshape(bf16[4,2,110592]{2,1,0:T(2,128)(2,1)S(1)} %all-to-all-done.1) | data formatting | bytes 3538944
  118.9 16.0 %reshape.174 = bf16[2048,3,6,24]{3,2,1,0:T(8,128)(2,1)} reshape(bf16[4,2,110592]{2,1,0:T(2,128)(2,1)S(1)} %all-to-all-done.2) | data formatting | bytes 3538944
  177.3 15.2 %reshape.171 = bf16[4,2,110592]{2,1,0:T(2,128)(2,1)} reshape(bf16[2048,3,6,24]{3,2,1,0:T(8,128)(2,1)} %bitcast.72) | data formatting | bytes 3538944
  200.4 27.9 %collective-permute-done = bf16[2,3,24,24,512]{4,3,2,1,0:T(8,128)(2,1)} collective-permute-done((bf16[2,3,24,24,512]{4,3,2,1,0:T(8,128)(2,1)}, bf16[2,3,24,24,512]{4,3,2,1,0:T(8,128)(2,1)}, u32[]{:S(2)}, u32[]{:S(2)}) %collective-permute-start) | collective-permute-done | bytes 3538976 | tf_op jit(solution)/shard_map/ppermute | solution.py:15
  236.3 16.9 %reshape.172 = bf16[2048,3,6,24]{3,2,1,0:T(8,128)(2,1)} reshape(bf16[4,2,110592]{2,1,0:T(2,128)(2,1)} %all-to-all-done) | data formatting | bytes 3538944
  272.0 32.2 %collective-permute-done.1 = bf16[2,3,24,24,512]{4,3,2,1,0:T(8,128)(2,1)} collective-permute-done((bf16[2,3,24,24,512]{4,3,2,1,0:T(8,128)(2,1)}, bf16[2,3,24,24,512]{4,3,2,1,0:T(8,128)(2,1)}, u32[]{:S(2)}, u32[]{:S(2)}) %collective-permute-start.1) | collective-permute-done | bytes 3538976 | tf_op jit(solution)/shard_map/ppermute | solution.py:15
  310.3 69.7 %collective-permute-done.3 = bf16[2,3,24,24,512]{4,3,2,1,0:T(8,128)(2,1)} collective-permute-done((bf16[2,3,24,24,512]{4,3,2,1,0:T(8,128)(2,1)}, bf16[2,3,24,24,512]{4,3,2,1,0:T(8,128)(2,1)}, u32[]{:S(2)}, u32[]{:S(2)}) %collective-permute-start.3) | collective-permute-done | bytes 3538976 | tf_op jit(solution)/shard_map/ppermute | solution.py:15
  382.2 77.6 %collective-permute-done.4 = bf16[2,3,24,24,512]{4,3,2,1,0:T(8,128)(2,1)} collective-permute-done((bf16[2,3,24,24,512]{4,3,2,1,0:T(8,128)(2,1)}, bf16[2,3,24,24,512]{4,3,2,1,0:T(8,128)(2,1)}, u32[]{:S(2)}, u32[]{:S(2)}) %collective-permute-start.4) | collective-permute-done | bytes 3538976 | tf_op jit(solution)/shard_map/ppermute | solution.py:15
  472.2 36.3 %reshape.130 = bf16[2,10368,4,128]{3,2,1,0:T(4,128)(2,1)} reshape(bf16[2,18,24,24,512]{4,3,2,1,0:T(8,128)(2,1)} %constant_dynamic-slice_fusion.1) | data formatting | bytes 42467328 | tf_op jit(solution)/shard_map/reshape | solution.py:23
  530.3 491.5 %while.14 = (s32[]{:T(128)}, bf16[9,4,192,128]{3,2,1,0:T(8,128)(2,1)S(1)}, s32[9]{0:T(128)S(1)}, bf16[4,3,24,24,128]{4,0,3,2,1:T(4,128)(2,1)}, bf16[4,10368,128]...) while((s32[]{:T(128)}, ...), condition=%wide.region_3.4_spmd.clone.clone, body=%wide.region_0.3_spmd.clone.clone.sunk | while | flops 4148805120 | bytes 198009328 | solution.py:62
  534.9 15.3 %fusion.29 = (f32[4,192]{1,0:T(4,128)S(1)}, f32[4,192,10368]{2,1,0:T(8,128)}) fusion(pred[10368]{0:T(1024)(128)(4,1)S(1)} %fusion.28, bf16[4,192,128]{2,1,0:T(8,128)(2,1)S(1)} %bitcast.73, bf16[4,10368,128]{2,1,0:T(8,128)(2,1)} %get-tuple-element.305), kind=kOutput, calls=%fused_computation.6.clone.1 | convolution fusion | flops 2062318848 | bytes 42677376 | tf_op jit(solution)/shard_map/while/body/eval_jaxpr/hqd,hkd->hqk/dot_general | solution.py:52
  589.5 15.3 %fusion.29 = (f32[4,192]{1,0:T(4,128)S(1)}, f32[4,192,10368]{2,1,0:T(8,128)}) fusion(pred[10368]{0:T(1024)(128)(4,1)S(1)} %fusion.28, bf16[4,192,128]{2,1,0:T(8,128)(2,1)S(1)} %bitcast.73, bf16[4,10368,128]{2,1,0:T(8,128)(2,1)} %get-tuple-element.305), kind=kOutput, calls=%fused_computation.6.clone.1 | convolution fusion | flops 2062318848 | bytes 42677376 | tf_op jit(solution)/shard_map/while/body/eval_jaxpr/hqd,hkd->hqk/dot_general | solution.py:52
  644.1 15.3 %fusion.29 = (f32[4,192]{1,0:T(4,128)S(1)}, f32[4,192,10368]{2,1,0:T(8,128)}) fusion(pred[10368]{0:T(1024)(128)(4,1)S(1)} %fusion.28, bf16[4,192,128]{2,1,0:T(8,128)(2,1)S(1)} %bitcast.73, bf16[4,10368,128]{2,1,0:T(8,128)(2,1)} %get-tuple-element.305), kind=kOutput, calls=%fused_computation.6.clone.1 | convolution fusion | flops 2062318848 | bytes 42677376 | tf_op jit(solution)/shard_map/while/body/eval_jaxpr/hqd,hkd->hqk/dot_general | solution.py:52
  698.6 15.3 %fusion.29 = (f32[4,192]{1,0:T(4,128)S(1)}, f32[4,192,10368]{2,1,0:T(8,128)}) fusion(pred[10368]{0:T(1024)(128)(4,1)S(1)} %fusion.28, bf16[4,192,128]{2,1,0:T(8,128)(2,1)S(1)} %bitcast.73, bf16[4,10368,128]{2,1,0:T(8,128)(2,1)} %get-tuple-element.305), kind=kOutput, calls=%fused_computation.6.clone.1 | convolution fusion | flops 2062318848 | bytes 42677376 | tf_op jit(solution)/shard_map/while/body/eval_jaxpr/hqd,hkd->hqk/dot_general | solution.py:52
  753.2 15.3 %fusion.29 = (f32[4,192]{1,0:T(4,128)S(1)}, f32[4,192,10368]{2,1,0:T(8,128)}) fusion(pred[10368]{0:T(1024)(128)(4,1)S(1)} %fusion.28, bf16[4,192,128]{2,1,0:T(8,128)(2,1)S(1)} %bitcast.73, bf16[4,10368,128]{2,1,0:T(8,128)(2,1)} %get-tuple-element.305), kind=kOutput, calls=%fused_computation.6.clone.1 | convolution fusion | flops 2062318848 | bytes 42677376 | tf_op jit(solution)/shard_map/while/body/eval_jaxpr/hqd,hkd->hqk/dot_general | solution.py:52
  807.8 15.3 %fusion.29 = (f32[4,192]{1,0:T(4,128)S(1)}, f32[4,192,10368]{2,1,0:T(8,128)}) fusion(pred[10368]{0:T(1024)(128)(4,1)S(1)} %fusion.28, bf16[4,192,128]{2,1,0:T(8,128)(2,1)S(1)} %bitcast.73, bf16[4,10368,128]{2,1,0:T(8,128)(2,1)} %get-tuple-element.305), kind=kOutput, calls=%fused_computation.6.clone.1 | convolution fusion | flops 2062318848 | bytes 42677376 | tf_op jit(solution)/shard_map/while/body/eval_jaxpr/hqd,hkd->hqk/dot_general | solution.py:52
  862.4 15.3 %fusion.29 = (f32[4,192]{1,0:T(4,128)S(1)}, f32[4,192,10368]{2,1,0:T(8,128)}) fusion(pred[10368]{0:T(1024)(128)(4,1)S(1)} %fusion.28, bf16[4,192,128]{2,1,0:T(8,128)(2,1)S(1)} %bitcast.73, bf16[4,10368,128]{2,1,0:T(8,128)(2,1)} %get-tuple-element.305), kind=kOutput, calls=%fused_computation.6.clone.1 | convolution fusion | flops 2062318848 | bytes 42677376 | tf_op jit(solution)/shard_map/while/body/eval_jaxpr/hqd,hkd->hqk/dot_general | solution.py:52
  877.7 13.6 %exponential_convert_fusion.2 = bf16[4,192,10368]{2,1,0:T(8,128)(2,1)S(1)} fusion(f32[4,192,10368]{2,1,0:T(8,128)} %get-tuple-element.267, f32[4,192]{1,0:T(4,128)S(1)} %get-tuple-element.268, pred[10368]{0:T(1024)(128)(4,1)S(1)} %fusion.28), kind=kLoop, calls=%fused_computation.4.clone.1 | loop fusion | flops 31850496 | bytes 47789184 | tf_op jit(solution)/shard_map/while/body/eval_jaxpr/convert_element_type | solution.py:57
  917.0 15.3 %fusion.29 = (f32[4,192]{1,0:T(4,128)S(1)}, f32[4,192,10368]{2,1,0:T(8,128)}) fusion(pred[10368]{0:T(1024)(128)(4,1)S(1)} %fusion.28, bf16[4,192,128]{2,1,0:T(8,128)(2,1)S(1)} %bitcast.73, bf16[4,10368,128]{2,1,0:T(8,128)(2,1)} %get-tuple-element.305), kind=kOutput, calls=%fused_computation.6.clone.1 | convolution fusion | flops 2062318848 | bytes 42677376 | tf_op jit(solution)/shard_map/while/body/eval_jaxpr/hqd,hkd->hqk/dot_general | solution.py:52
  971.6 15.3 %fusion.29 = (f32[4,192]{1,0:T(4,128)S(1)}, f32[4,192,10368]{2,1,0:T(8,128)}) fusion(pred[10368]{0:T(1024)(128)(4,1)S(1)} %fusion.28, bf16[4,192,128]{2,1,0:T(8,128)(2,1)S(1)} %bitcast.73, bf16[4,10368,128]{2,1,0:T(8,128)(2,1)} %get-tuple-element.305), kind=kOutput, calls=%fused_computation.6.clone.1 | convolution fusion | flops 2062318848 | bytes 42677376 | tf_op jit(solution)/shard_map/while/body/eval_jaxpr/hqd,hkd->hqk/dot_general | solution.py:52
  1022.3 40.7 %all_to_all.63 = bf16[3,24,24,512]{3,2,0,1:T(8,128)(2,1)S(1)} all-to-all(bf16[3,24,24,512]{3,2,0,1:T(8,128)(2,1)S(1)} %copy.28), channel_id=1, replica_groups=mesh['tm'=8,'height'=4] {'height'}, dimensions={1} | all-to-all | bytes 3538944 | tf_op jit(solution)/shard_map/all_to_all | solution.py:94
  (182 shorter events, 502.9 us)
Async XLA Ops:
  13.1 20.2 %copy-start.1 = (bf16[3,6,24,2048]{3,2,1,0:T(8,128)(2,1)S(1)}, bf16[3,6,24,2048]{3,2,1,0:T(8,128)(2,1)}, u32[]{:S(2)}) copy-start(bf16[3,6,24,2048]{3,2,1,0:T(8,128)(2,1)} %param.7) | copy-start | bytes 5308420
  28.4 46.0 %all-to-all-start.1 = ((bf16[4,2,110592]{2,1,0:T(2,128)(2,1)}), bf16[4,2,110592]{2,1,0:T(2,128)(2,1)S(1)}, u32[]{:S(2)}, u32[]{:S(2)}) async-start(bf16[4,2,110592]{2,1,0:T(2,128)(2,1)} %reshape.175), calls=%async_computation.1 | async-start | bytes 3538944 | tf_op jit(solution)/shard_map/all_to_all | solution.py:75
  74.5 44.4 %all-to-all-start.2 = ((bf16[4,2,110592]{2,1,0:T(2,128)(2,1)}), bf16[4,2,110592]{2,1,0:T(2,128)(2,1)S(1)}, u32[]{:S(2)}, u32[]{:S(2)}) async-start(bf16[4,2,110592]{2,1,0:T(2,128)(2,1)} %reshape.173), calls=%async_computation.2 | async-start | bytes 3538944 | tf_op jit(solution)/shard_map/all_to_all | solution.py:76
  151.7 76.6 %collective-permute-start = (bf16[2,3,24,24,512]{4,3,2,1,0:T(8,128)(2,1)}, bf16[2,3,24,24,512]{4,3,2,1,0:T(8,128)(2,1)}, u32[]{:S(2)}, u32[]{:S(2)}) collective-permute-start(bf16[2,3,24,24,512]{4,3,2,1,0:T(8,128)(2,1)} %pad_maximum_fusion), channel_id=1, source_target_pairs={{0,12},{4,16},{8,20},{12,24},{16,28},{1,13},{5,17},{9,21},{13,25},... | collective-permute-start | bytes 10616840 | tf_op jit(solution)/shard_map/ppermute | solution.py:15
  155.6 148.6 %collective-permute-start.1 = (bf16[2,3,24,24,512]{4,3,2,1,0:T(8,128)(2,1)}, bf16[2,3,24,24,512]{4,3,2,1,0:T(8,128)(2,1)}, u32[]{:S(2)}, u32[]{:S(2)}) collective-permute-start(bf16[2,3,24,24,512]{4,3,2,1,0:T(8,128)(2,1)} %pad_maximum_fusion), channel_id=1, source_target_pairs={{0,8},{4,12},{8,16},{12,20},{16,24},{20,28},{1,9},{5,13},{9,17},{1... | collective-permute-start | bytes 10616840 | tf_op jit(solution)/shard_map/ppermute | solution.py:15
  157.5 150.3 %collective-permute-start.2 = (bf16[2,3,24,24,512]{4,3,2,1,0:T(8,128)(2,1)}, bf16[2,3,24,24,512]{4,3,2,1,0:T(8,128)(2,1)}, u32[]{:S(2)}, u32[]{:S(2)}) collective-permute-start(bf16[2,3,24,24,512]{4,3,2,1,0:T(8,128)(2,1)} %pad_maximum_fusion), channel_id=1, source_target_pairs={{0,4},{4,8},{8,12},{12,16},{16,20},{20,24},{24,28},{1,5},{5,9},{9,... | collective-permute-start | bytes 10616840 | tf_op jit(solution)/shard_map/ppermute | solution.py:15
  159.4 220.6 %collective-permute-start.3 = (bf16[2,3,24,24,512]{4,3,2,1,0:T(8,128)(2,1)}, bf16[2,3,24,24,512]{4,3,2,1,0:T(8,128)(2,1)}, u32[]{:S(2)}, u32[]{:S(2)}) collective-permute-start(bf16[2,3,24,24,512]{4,3,2,1,0:T(8,128)(2,1)} %pad_maximum_fusion), channel_id=1, source_target_pairs={{4,0},{8,4},{12,8},{16,12},{20,16},{24,20},{28,24},{5,1},{9,5},{13... | collective-permute-start | bytes 10616840 | tf_op jit(solution)/shard_map/ppermute | solution.py:15
  192.5 43.8 %all-to-all-start = ((bf16[4,2,110592]{2,1,0:T(2,128)(2,1)}), bf16[4,2,110592]{2,1,0:T(2,128)(2,1)}, u32[]{:S(2)}, u32[]{:S(2)}) async-start(bf16[4,2,110592]{2,1,0:T(2,128)(2,1)} %reshape.171), calls=%async_computation | async-start | bytes 3538944 | tf_op jit(solution)/shard_map/all_to_all | solution.py:74
  196.9 262.9 %collective-permute-start.4 = (bf16[2,3,24,24,512]{4,3,2,1,0:T(8,128)(2,1)}, bf16[2,3,24,24,512]{4,3,2,1,0:T(8,128)(2,1)}, u32[]{:S(2)}, u32[]{:S(2)}) collective-permute-start(bf16[2,3,24,24,512]{4,3,2,1,0:T(8,128)(2,1)} %pad_maximum_fusion), channel_id=1, source_target_pairs={{8,0},{12,4},{16,8},{20,12},{24,16},{28,20},{9,1},{13,5},{17,9},{2... | collective-permute-start | bytes 10616840 | tf_op jit(solution)/shard_map/ppermute | solution.py:15
  228.3 233.7 %collective-permute-start.5 = (bf16[2,3,24,24,512]{4,3,2,1,0:T(8,128)(2,1)}, bf16[2,3,24,24,512]{4,3,2,1,0:T(8,128)(2,1)}, u32[]{:S(2)}, u32[]{:S(2)}) collective-permute-start(bf16[2,3,24,24,512]{4,3,2,1,0:T(8,128)(2,1)} %pad_maximum_fusion), channel_id=1, source_target_pairs={{12,0},{16,4},{20,8},{24,12},{28,16},{13,1},{17,5},{21,9},{25,13},... | collective-permute-start | bytes 10616840 | tf_op jit(solution)/shard_map/ppermute | solution.py:15
  524.3 6.0 copy-start.2
  563.8 5.5 copy-start
  618.4 5.5 copy-start
  673.0 5.5 copy-start
  727.6 5.5 copy-start
  782.2 5.5 copy-start
  836.8 5.5 copy-start
  891.3 5.5 copy-start
  945.9 5.5 copy-start
  1000.5 5.5 copy-start
where the time goes:
time: 1080 us; the launch traced here: 1070 us
  local copies, waits for them, and re-layouts  333 us (31%)
  matrix products  254 us (24%)
  waiting for transfers between devices  237 us (22%)
  other arithmetic  153 us (14%)
  blocking collectives  40.7 us (4%)
  starting transfers between devices  30.4 us (3%)
  loops' own time  18.9 us (2%)
    ppermute x6, waiting for transfers between devices, from_behind(): lax.ppermute(value, axis, [(source, source + steps) for source in range(l...  209 us
    unnamed x20, local copies, waits for them, and re-layouts  155 us
    dot_general x9, matrix products, one_tile(): jnp.einsum('hqd,hkd->hqk', query_block, key_rows, preferred_element_type=...  138 us
    convert_element_type x9, other arithmetic, one_tile(): jnp.exp(scores - largest).astype(jnp.bfloat16)  123 us
    dot_general x9, matrix products, one_tile(): jnp.einsum('hqk,hkd->hqd', weights, value_rows, preferred_element_type=jn...  116 us
    while x18, local copies, waits for them, and re-layouts  49.7 us
    all_to_all x1, blocking collectives, body(): lax.all_to_all(attended_heads, 'height', split_axis=1, concat_axis=3, til...  40.7 us
    reshape x1, local copies, waits for them, and re-layouts, attend_plane(): window.reshape(2, key_count, local_heads, HEAD_DIM)  36.3 us
  transfers between devices with their start and end apart: 9, of which 8 were waited for; matrix products, arithmetic and copies ran while one was open for 12% of the time, Pallas kernels for 0%

commit v1 on v0

v1 whole, which is shorter than its diff:
```python
import functools
import math

import jax
import jax.numpy as jnp
from jax import lax
from jax.experimental import pallas as pl
from jax.experimental.pallas import tpu as pltpu
from jax.sharding import PartitionSpec as P

HEAD_DIM = 128
TILE_T = 6
TILE_H = 8
TILE_W = 8
MESH = pl.DeviceIdType.MESH

KEY_BLOCK = (0, 1, 5)
VALUE_BLOCK = (2, 3, 6)
QUERY_BLOCK = (4, 7, 8)
ORDER = (("k", 0), ("k", 1), ("v", 0), ("v", 1), ("q", 0), ("k", 2), ("v", 2), ("q", 1), ("q", 2))
PHASES = ((0, 5), (5, 4))
HALO = ((0, 4), (5, 2))


def kernel(dims, x_ref, out_ref, y, o, scores, send, recv, osend, orecv, hsend, hrecv):
    heads, tm, height, frames, rows, tall = dims
    heads_here = heads // height
    group = tm // heads_here
    own = heads_here
    tiles = own * frames // TILE_T
    piece = frames * rows * TILE_W
    unit = frames * TILE_H * TILE_W
    scale = HEAD_DIM ** (-0.5) * math.log2(math.e)

    me_t, me_z = lax.axis_index("tm"), lax.axis_index("height")
    part = lax.rem(me_t, group)
    my_head = me_z * heads_here + me_t // group
    my_part = me_t // own
    my_slot = lax.rem(me_t, own)
    me = me_t * height + me_z

    barrier = pltpu.get_barrier_semaphore()

    def greet(step, carry):
        other = lax.rem(me + step, tm * height)
        pl.semaphore_signal(
            barrier,
            inc=1,
            device_id={"tm": other // height, "height": lax.rem(other, height)},
            device_id_type=MESH,
        )
        return carry

    lax.fori_loop(1, tm * height, greet, 0)
    pl.semaphore_wait(barrier, tm * height - 1)

    def sending(phase, head):
        first, count = PHASES[phase]
        return pltpu.make_async_remote_copy(
            src_ref=x_ref.at[head, pl.ds(first, count)],
            dst_ref=y.at[pl.ds(first, count), 2 + my_slot, pl.ds(me_z * piece, piece), :],
            send_sem=send.at[phase, head],
            recv_sem=recv.at[phase, my_slot * height + me_z],
            device_id={"tm": lax.rem(head, heads_here) * group + my_part, "height": head // heads_here},
            device_id_type=MESH,
        )

    def keeping(phase):
        first, count = PHASES[phase]
        return pltpu.make_async_copy(
            x_ref.at[my_head, pl.ds(first, count)],
            y.at[pl.ds(first, count), 2 + my_slot, pl.ds(me_z * piece, piece), :],
            recv.at[phase, my_slot * height + me_z],
        )

    def is_me(head):
        return (head == my_head) & (part == my_part)

    def start_phase(phase):
        def one(step, carry):
            head = lax.rem(my_head + step, heads)

            @pl.when(jnp.logical_not(is_me(head)))
            def _():
                sending(phase, head).start()

            @pl.when(is_me(head))
            def _():
                keeping(phase).start()

            return carry

        lax.fori_loop(0, heads, one, 0)

    def finish_sends(phase):
        def one(head, carry):
            @pl.when(jnp.logical_not(is_me(head)))
            def _():
                sending(phase, head).wait_send()

            return carry

        lax.fori_loop(0, heads, one, 0)

    def receive_phase(phase):
        first, count = PHASES[phase]

        def one(source, carry):
            slot, z = source // height, lax.rem(source, height)
            mine = (part * own + slot == me_t) & (z == me_z)

            @pl.when(mine)
            def _():
                keeping(phase).wait()

            @pl.when(jnp.logical_not(mine))
            def _():
                pltpu.make_async_remote_copy(
                    src_ref=x_ref.at[0, pl.ds(first, count)],
                    dst_ref=y.at[pl.ds(first, count), 2 + slot, pl.ds(z * piece, piece), :],
                    send_sem=send.at[phase, 0],
                    recv_sem=recv.at[phase, source],
                    device_id={"tm": part * own + slot, "height": z},
                    device_id_type=MESH,
                ).wait_recv()

            return carry

        lax.fori_loop(0, own * height, one, 0)

    def halo(phase, right):
        first, count = HALO[phase]
        source, target, to = (own, 0, me_t + 1) if right else (2, own + 2, me_t - 1)
        return pltpu.make_async_remote_copy(
            src_ref=y.at[pl.ds(first, count), pl.ds(source, 2)],
            dst_ref=y.at[pl.ds(first, count), pl.ds(target, 2)],
            send_sem=hsend.at[phase, int(right)],
            recv_sem=hrecv.at[phase, int(right)],
            device_id={"tm": to},
            device_id_type=MESH,
        )

    def exchange_halo(phase):
        @pl.when(part < group - 1)
        def _():
            halo(phase, True).start()

        @pl.when(part > 0)
        def _():
            halo(phase, False).start()

        @pl.when(part < group - 1)
        def _():
            halo(phase, False).wait_recv()

        @pl.when(part > 0)
        def _():
            halo(phase, True).wait_recv()

    def finish_halo(phase):
        @pl.when(part < group - 1)
        def _():
            halo(phase, True).wait_send()

        @pl.when(part > 0)
        def _():
            halo(phase, False).wait_send()

    def attend(column, row, span, tile):
        columns = (max(column - 1, 0), min(column + 2, 3))
        first_pair = tile + jnp.where((part == 0) & (tile == 0), 1, 0)
        last_pair = tile + jnp.where((part == group - 1) & (tile == tiles - 1), 2, 3)
        width = 2 * span * unit
        at = pl.ds(pl.multiple_of(row * unit, unit), unit)
        near = pl.ds(pl.multiple_of(jnp.maximum(row - 1, 0) * unit, unit), span * unit)
        query = jnp.concatenate(
            [y[QUERY_BLOCK[column], 2 + 2 * tile + half, at, :] for half in (0, 1)], axis=0
        )

        def pair_of(block, pair):
            return jnp.concatenate([y[block, 2 * pair + half, near, :] for half in (0, 1)], axis=0)

        def place(c, pair):
            return (c - columns[0]) * 3 + pair - tile

        def score(c, largest):
            block = jnp.where(c == 2, KEY_BLOCK[2], c)

            def one(pair, largest):
                found = lax.dot_general(
                    query, pair_of(block, pair), (((1,), (1,)), ((), ())),
                    preferred_element_type=jnp.float32,
                )
                scores[place(c, pair), :, :width] = found
                for lane in range(0, width, 128):
                    largest = jnp.maximum(largest, found[:, lane : lane + 128])
                return largest

            return lax.fori_loop(first_pair, last_pair, one, largest)

        lowest = jnp.full((2 * unit, 128), -jnp.inf, jnp.float32)
        largest = lax.fori_loop(columns[0], columns[1], score, lowest)
        largest = jnp.max(largest, axis=1, keepdims=True)
        ones = jnp.ones((width, 128), jnp.bfloat16)

        def add(c, total):
            block = jnp.where(c == 2, VALUE_BLOCK[2], c + VALUE_BLOCK[0])

            def one(pair, total):
                weights = jnp.exp2((scores[place(c, pair), :, :width] - largest) * scale)
                value = jnp.concatenate([pair_of(block, pair), ones], axis=1)
                return total + jnp.dot(
                    weights.astype(jnp.bfloat16), value, preferred_element_type=jnp.float32
                )

            return lax.fori_loop(first_pair, last_pair, one, total)

        total = lax.fori_loop(columns[0], columns[1], add, jnp.zeros((2 * unit, 256), jnp.float32))
        result = (total[:, :128] / total[:, 128:]).astype(o.dtype)
        for half in (0, 1):
            o[column, 2 * tile + half, at, :] = result[half * unit : (half + 1) * unit]

    def attend_column(column):
        def one(step, carry):
            tile = jnp.where(lax.rem(part, 2) == 0, step, tiles - 1 - step)
            row_tiles = tall // TILE_H

            def edge(which, carry):
                attend(column, which * (row_tiles - 1), 2, tile)
                return carry

            def inner(row, carry):
                attend(column, row, 3, tile)
                return carry

            lax.fori_loop(0, 2, edge, 0)
            lax.fori_loop(1, row_tiles - 1, inner, 0)
            return carry

        lax.fori_loop(0, tiles, one, 0)

    def returning(column, source):
        slot, z = source // height, lax.rem(source, height)
        return pltpu.make_async_remote_copy(
            src_ref=o.at[column, slot, pl.ds(z * piece, piece), :],
            dst_ref=out_ref.at[my_head, column],
            send_sem=osend.at[column, source],
            recv_sem=orecv.at[column, my_head],
            device_id={"tm": part * own + slot, "height": z},
            device_id_type=MESH,
        )

    def returning_here(column):
        return pltpu.make_async_copy(
            o.at[column, my_slot, pl.ds(me_z * piece, piece), :],
            out_ref.at[my_head, column],
            orecv.at[column, my_head],
        )

    def source_is_me(source):
        return (part * own + source // height == me_t) & (lax.rem(source, height) == me_z)

    def return_column(column):
        def one(step, carry):
            source = lax.rem(my_slot * height + me_z + step, own * height)

            @pl.when(jnp.logical_not(source_is_me(source)))
            def _():
                returning(column, source).start()

            @pl.when(source_is_me(source))
            def _():
                returning_here(column).start()

            return carry

        lax.fori_loop(0, own * height, one, 0)

    def finish_column(column):
        def sent(source, carry):
            @pl.when(jnp.logical_not(source_is_me(source)))
            def _():
                returning(column, source).wait_send()

            return carry

        lax.fori_loop(0, own * height, sent, 0)

        def landed(head, carry):
            @pl.when(is_me(head))
            def _():
                returning_here(column).wait()

            @pl.when(jnp.logical_not(is_me(head)))
            def _():
                pltpu.make_async_remote_copy(
                    src_ref=o.at[column, 0, pl.ds(0, piece), :],
                    dst_ref=out_ref.at[head, column],
                    send_sem=osend.at[column, 0],
                    recv_sem=orecv.at[column, head],
                    device_id={"tm": lax.rem(head, heads_here) * group + my_part, "height": head // heads_here},
                    device_id_type=MESH,
                ).wait_recv()

            return carry

        lax.fori_loop(0, heads, landed, 0)

    for phase in (0, 1):
        start_phase(phase)
    receive_phase(0)
    exchange_halo(0)
    attend_column(0)
    return_column(0)
    receive_phase(1)
    exchange_halo(1)
    attend_column(1)
    return_column(1)
    attend_column(2)
    return_column(2)
    for phase in (0, 1):
        finish_sends(phase)
        finish_halo(phase)
    for column in (0, 1, 2):
        finish_column(column)


def body(query_band, key_band, value_band):
    frames, rows, cols, features = query_band.shape
    heads = features // HEAD_DIM
    tm, height = lax.axis_size("tm"), lax.axis_size("height")
    columns = cols // TILE_W
    piece = frames * rows * TILE_W
    tall = rows * height
    own = heads // height

    def by_head(value):
        value = value.reshape(frames, rows, columns, TILE_W, heads, HEAD_DIM)
        return jnp.transpose(value, (4, 2, 1, 0, 3, 5)).reshape(heads, columns, piece, HEAD_DIM)

    bands = {"q": by_head(query_band), "k": by_head(key_band), "v": by_head(value_band)}
    blocks = jnp.stack([bands[name][:, column] for name, column in ORDER], axis=1)

    unit = frames * TILE_H * TILE_W
    dims = (heads, tm, height, frames, rows, tall)
    result = pl.pallas_call(
        functools.partial(kernel, dims),
        out_shape=jax.ShapeDtypeStruct((heads, columns, piece, HEAD_DIM), jnp.bfloat16),
        in_specs=[pl.BlockSpec(memory_space=pl.ANY)],
        out_specs=pl.BlockSpec(memory_space=pl.ANY),
        scratch_shapes=[
            pltpu.VMEM((3 * columns, own + 4, piece * height, HEAD_DIM), jnp.bfloat16),
            pltpu.VMEM((columns, own, piece * height, HEAD_DIM), jnp.bfloat16),
            pltpu.VMEM((9, 2 * unit, 6 * unit), jnp.float32),
            pltpu.SemaphoreType.DMA((2, heads)),
            pltpu.SemaphoreType.DMA((2, own * height)),
            pltpu.SemaphoreType.DMA((columns, own * height)),
            pltpu.SemaphoreType.DMA((columns, heads)),
            pltpu.SemaphoreType.DMA((2, 2)),
            pltpu.SemaphoreType.DMA((2, 2)),
        ],
        compiler_params=pltpu.CompilerParams(
            collective_id=0, has_side_effects=True, vmem_limit_bytes=56 * 1024 * 1024
        ),
    )(blocks)
    result = result.reshape(heads, columns, rows, frames, TILE_W, HEAD_DIM)
    return jnp.transpose(result, (3, 2, 1, 4, 0, 5)).reshape(frames, rows, cols, features)


def solution(mesh):
    band = P("tm", "height", None, None)
    return jax.shard_map(
        body,
        mesh=mesh,
        in_specs=(band, band, band),
        out_specs=band,
        check_vma=False,
    )
```

time: 1080 us -> 224 us (0.21); the launches traced: 1070 us -> 223 us
  local copies, waits for them, and re-layouts: 333 us -> 10.1 us
  matrix products: 254 us -> 0 us
  waiting for transfers between devices: 237 us -> 0 us
  Pallas kernels: 0 us -> 213 us
  other arithmetic: 153 us -> 0 us
  blocking collectives: 40.7 us -> 0 us
  starting transfers between devices: 30.4 us -> 0 us
  loops' own time: 18.9 us -> 0 us
    dot_general x18 -> x0, matrix products: 254 us -> none  [the longest x9 138 us: one_tile(): jnp.einsum('hqd,hkd->hqk', query_block, key_rows, preferred_element_type=...]
    pallas_call x0 -> x1, Pallas kernels: none -> 213 us  [body(): pl.pallas_call(functools.partial(kernel, dims), out_shape=jax.ShapeDtypeS...]
    ppermute x6 -> x0, waiting for transfers between devices: 209 us -> none  [from_behind(): lax.ppermute(value, axis, [(source, source + steps) for source in range(l...]
    unnamed x20 -> x9, local copies, waits for them, and re-layouts: 155 us -> 2.78 us
    convert_element_type x9 -> x0, other arithmetic: 123 us -> none  [one_tile(): jnp.exp(scores - largest).astype(jnp.bfloat16)]
    while x18 -> x0, local copies, waits for them, and re-layouts: 49.7 us -> none
    all_to_all x7 -> x0, local copies, waits for them, and re-layouts: 45.9 us -> none  [the longest x2 14.8 us: body(): lax.all_to_all(key_band, 'height', split_axis=3, concat_axis=1, tiled=True)]
    all_to_all x1 -> x0, blocking collectives: 40.7 us -> none  [body(): lax.all_to_all(attended_heads, 'height', split_axis=1, concat_axis=3, til...]
  transfers between devices with their start and end apart: 9 -> 0, of which waited for: 8 -> 0; matrix products, arithmetic and copies ran while one was open for 12% -> 0% of each run, Pallas kernels for 0% -> 0%
where the time goes in v1:
time: 224 us; the launch traced here: 223 us
  Pallas kernels  213 us (95%)
  local copies, waits for them, and re-layouts  10.1 us (5%)
    pallas_call x1, Pallas kernels, body(): pl.pallas_call(functools.partial(kernel, dims), out_shape=jax.ShapeDtypeS...  213 us

profile of v1, /device:TPU:2, one launch (start us, length us, event | category | flops | bytes accessed | tf_op | source)
XLA Modules:
  0.0 223.1 jit_solution(8507276375512880885)
XLA Ops:
  0.0 0.0 copy-start.1
  0.0 1.9 copy.6
  1.9 1.8 copy.4
  3.7 0.0 copy-done.1
  3.7 0.3 copy.5
  4.0 0.1 slice_dynamic-update-slice_fusion.2
  4.1 0.2 slice_dynamic-update-slice_fusion.1
  4.3 0.1 slice_dynamic-update-slice_fusion.5
  4.4 0.1 slice_dynamic-update-slice_fusion.4
  4.4 0.1 slice_dynamic-update-slice_fusion.3
  4.5 0.2 slice_dynamic-update-slice_fusion.x_ref
  4.7 0.0 copy-start
  4.7 2.3 %copy-done = bf16[16,9,144,128]{3,2,1,0:T(8,128)(2,1)} copy-done((bf16[16,9,144,128]{3,2,1,0:T(8,128)(2,1)}, bf16[16,9,144,128]{3,2,1,0:T(8,128)(2,1)S(1)}, u32[]{:S(2)}) %copy-start) | copy-done | bytes 5308440
  7.0 212.9 %shard_map.37 = bf16[16,3,144,128]{3,2,1,0:T(8,128)(2,1)} custom-call(bf16[16,9,144,128]{3,2,1,0:T(8,128)(2,1)} %copy-done), custom_call_target="tpu_custom_call" | custom-call | tf_op jit(solution)/shard_map/pallas_call | solution.py:346
  219.9 3.2 %copy.9 = bf16[3,6,3,8,16,128]{5,3,4,2,1,0:T(8,128)(2,1)} copy(bf16[3,6,3,8,16,128]{5,3,0,1,2,4:T(8,128)(2,1)} %bitcast.18) | data formatting | bytes 3538944 | tf_op jit(solution)/shard_map/transpose | solution.py:367
Async XLA Ops:
  0.0 3.7 %copy-start.1 = (bf16[3,6,24,2048]{3,2,1,0:T(8,128)(2,1)S(1)}, bf16[3,6,24,2048]{3,2,1,0:T(8,128)(2,1)}, u32[]{:S(2)}) copy-start(bf16[3,6,24,2048]{3,2,1,0:T(8,128)(2,1)} %param.5) | copy-start | bytes 5308420
  4.7 2.3 %copy-start = (bf16[16,9,144,128]{3,2,1,0:T(8,128)(2,1)}, bf16[16,9,144,128]{3,2,1,0:T(8,128)(2,1)S(1)}, u32[]{:S(2)}) copy-start(bf16[16,9,144,128]{3,2,1,0:T(8,128)(2,1)S(1)} %slice_dynamic-update-slice_fusion.x_ref) | copy-start | bytes 15925252

commit v2 on v1

--- a/solution.py
+++ b/solution.py
@@ -18,7 +18,7 @@
 VALUE_BLOCK = (2, 3, 6)
 QUERY_BLOCK = (4, 7, 8)
 ORDER = (("k", 0), ("k", 1), ("v", 0), ("v", 1), ("q", 0), ("k", 2), ("v", 2), ("q", 1), ("q", 2))
-PHASES = ((0, 5), (5, 4))
+PHASES = ((0, 5), (5, 3), (8, 1))
 HALO = ((0, 4), (5, 2))
 
 
@@ -38,6 +38,7 @@
     my_part = me_t // own
     my_slot = lax.rem(me_t, own)
     me = me_t * height + me_z
+    hops = sorted(range(height), key=lambda hop: abs(hop - height / 2))
 
     barrier = pltpu.get_barrier_semaphore()
 
@@ -78,19 +79,21 @@
 
     def start_phase(phase):
         def one(step, carry):
-            head = lax.rem(my_head + step, heads)
-
-            @pl.when(jnp.logical_not(is_me(head)))
-            def _():
-                sending(phase, head).start()
-
-            @pl.when(is_me(head))
-            def _():
-                keeping(phase).start()
-
-            return carry
-
-        lax.fori_loop(0, heads, one, 0)
+            chip = lax.rem(me_t // group + step, heads_here)
+            for hop in hops:
+                head = lax.rem(me_z + hop, height) * heads_here + chip
+
+                @pl.when(jnp.logical_not(is_me(head)))
+                def _():
+                    sending(phase, head).start()
+
+                @pl.when(is_me(head))
+                def _():
+                    keeping(phase).start()
+
+            return carry
+
+        lax.fori_loop(0, heads_here, one, 0)
 
     def finish_sends(phase):
         def one(head, carry):
@@ -235,6 +238,7 @@
 
             lax.fori_loop(0, 2, edge, 0)
             lax.fori_loop(1, row_tiles - 1, inner, 0)
+            return_tile(column, tile)
             return carry
 
         lax.fori_loop(0, tiles, one, 0)
@@ -260,9 +264,10 @@
     def source_is_me(source):
         return (part * own + source // height == me_t) & (lax.rem(source, height) == me_z)
 
-    def return_column(column):
+    def return_tile(column, tile):
         def one(step, carry):
-            source = lax.rem(my_slot * height + me_z + step, own * height)
+            z = lax.rem(me_z + height // 2 + step // 2, height)
+            source = (2 * tile + lax.rem(step, 2)) * height + z
 
             @pl.when(jnp.logical_not(source_is_me(source)))
             def _():
@@ -274,7 +279,7 @@
 
             return carry
 
-        lax.fori_loop(0, own * height, one, 0)
+        lax.fori_loop(0, 2 * height, one, 0)
 
     def finish_column(column):
         def sent(source, carry):
@@ -306,20 +311,16 @@
 
         lax.fori_loop(0, heads, landed, 0)
 
-    for phase in (0, 1):
+    for phase in range(len(PHASES)):
         start_phase(phase)
-    receive_phase(0)
-    exchange_halo(0)
-    attend_column(0)
-    return_column(0)
-    receive_phase(1)
-    exchange_halo(1)
-    attend_column(1)
-    return_column(1)
-    attend_column(2)
-    return_column(2)
-    for phase in (0, 1):
+    for phase in range(len(PHASES)):
+        receive_phase(phase)
+        if phase < len(HALO):
+            exchange_halo(phase)
+        attend_column(phase)
+    for phase in range(len(PHASES)):
         finish_sends(phase)
+    for phase in range(len(HALO)):
         finish_halo(phase)
     for column in (0, 1, 2):
         finish_column(column)
@@ -352,8 +353,8 @@
             pltpu.VMEM((3 * columns, own + 4, piece * height, HEAD_DIM), jnp.bfloat16),
             pltpu.VMEM((columns, own, piece * height, HEAD_DIM), jnp.bfloat16),
             pltpu.VMEM((9, 2 * unit, 6 * unit), jnp.float32),
-            pltpu.SemaphoreType.DMA((2, heads)),
-            pltpu.SemaphoreType.DMA((2, own * height)),
+            pltpu.SemaphoreType.DMA((len(PHASES), heads)),
+            pltpu.SemaphoreType.DMA((len(PHASES), own * height)),
             pltpu.SemaphoreType.DMA((columns, own * height)),
             pltpu.SemaphoreType.DMA((columns, heads)),
             pltpu.SemaphoreType.DMA((2, 2)),

time: 224 us -> 206 us (0.920)
  Pallas kernels: 213 us -> 195 us
    pallas_call x1, Pallas kernels: 213 us -> 195 us  [body(): pl.pallas_call(functools.partial(kernel, dims), out_shape=jax.ShapeDtypeS...]
where the time goes in v2:
time: 206 us; the launch traced here: 205 us
  Pallas kernels  195 us (95%)
  local copies, waits for them, and re-layouts  10.1 us (5%)
    pallas_call x1, Pallas kernels, body(): pl.pallas_call(functools.partial(kernel, dims), out_shape=jax.ShapeDtypeS...  195 us

profile of v2, /device:TPU:2, one launch (start us, length us, event | category | flops | bytes accessed | tf_op | source)
XLA Modules:
  0.0 205.2 jit_solution(15442784383957614436)
XLA Ops:
  0.0 0.0 copy-start.1
  0.0 1.9 copy.6
  1.9 1.8 copy.4
  3.7 0.0 copy-done.1
  3.7 0.3 copy.5
  4.0 0.1 slice_dynamic-update-slice_fusion.2
  4.1 0.2 slice_dynamic-update-slice_fusion.1
  4.3 0.1 slice_dynamic-update-slice_fusion.5
  4.4 0.1 slice_dynamic-update-slice_fusion.4
  4.4 0.1 slice_dynamic-update-slice_fusion.3
  4.5 0.2 slice_dynamic-update-slice_fusion.x_ref
  4.7 0.0 copy-start
  4.7 2.3 %copy-done = bf16[16,9,144,128]{3,2,1,0:T(8,128)(2,1)} copy-done((bf16[16,9,144,128]{3,2,1,0:T(8,128)(2,1)}, bf16[16,9,144,128]{3,2,1,0:T(8,128)(2,1)S(1)}, u32[]{:S(2)}) %copy-start) | copy-done | bytes 5308440
  7.0 195.0 %shard_map.37 = bf16[16,3,144,128]{3,2,1,0:T(8,128)(2,1)} custom-call(bf16[16,9,144,128]{3,2,1,0:T(8,128)(2,1)} %copy-done), custom_call_target="tpu_custom_call" | custom-call | tf_op jit(solution)/shard_map/pallas_call | solution.py:347
  202.0 3.2 %copy.9 = bf16[3,6,3,8,16,128]{5,3,4,2,1,0:T(8,128)(2,1)} copy(bf16[3,6,3,8,16,128]{5,3,0,1,2,4:T(8,128)(2,1)} %bitcast.18) | data formatting | bytes 3538944 | tf_op jit(solution)/shard_map/transpose | solution.py:368
Async XLA Ops:
  0.0 3.7 %copy-start.1 = (bf16[3,6,24,2048]{3,2,1,0:T(8,128)(2,1)S(1)}, bf16[3,6,24,2048]{3,2,1,0:T(8,128)(2,1)}, u32[]{:S(2)}) copy-start(bf16[3,6,24,2048]{3,2,1,0:T(8,128)(2,1)} %param.5) | copy-start | bytes 5308420
  4.7 2.3 %copy-start = (bf16[16,9,144,128]{3,2,1,0:T(8,128)(2,1)}, bf16[16,9,144,128]{3,2,1,0:T(8,128)(2,1)S(1)}, u32[]{:S(2)}) copy-start(bf16[16,9,144,128]{3,2,1,0:T(8,128)(2,1)S(1)} %slice_dynamic-update-slice_fusion.x_ref) | copy-start | bytes 15925252

commit v3 on v2

--- a/solution.py
+++ b/solution.py
@@ -12,6 +12,7 @@
 TILE_T = 6
 TILE_H = 8
 TILE_W = 8
+BLOCK = 768
 MESH = pl.DeviceIdType.MESH
 
 KEY_BLOCK = (0, 1, 5)
@@ -183,42 +184,40 @@
         def pair_of(block, pair):
             return jnp.concatenate([y[block, 2 * pair + half, near, :] for half in (0, 1)], axis=0)
 
-        def place(c, pair):
-            return (c - columns[0]) * 3 + pair - tile
-
-        def score(c, largest):
-            block = jnp.where(c == 2, KEY_BLOCK[2], c)
-
-            def one(pair, largest):
+        across = range(columns[0], columns[1])
+        blocks = [(low, min(low + BLOCK, width * len(across))) for low in range(0, width * len(across), BLOCK)]
+
+        def score(pair, largest):
+            keys = jnp.concatenate([pair_of(KEY_BLOCK[c], pair) for c in across], axis=0)
+            for low, high in blocks:
                 found = lax.dot_general(
-                    query, pair_of(block, pair), (((1,), (1,)), ((), ())),
-                    preferred_element_type=jnp.float32,
+                    query, keys[low:high], (((1,), (1,)), ((), ())), preferred_element_type=jnp.float32
                 )
-                scores[place(c, pair), :, :width] = found
-                for lane in range(0, width, 128):
+                scores[pair - tile, :, low:high] = found
+                for lane in range(0, high - low, 128):
                     largest = jnp.maximum(largest, found[:, lane : lane + 128])
-                return largest
-
-            return lax.fori_loop(first_pair, last_pair, one, largest)
+            return largest
 
         lowest = jnp.full((2 * unit, 128), -jnp.inf, jnp.float32)
-        largest = lax.fori_loop(columns[0], columns[1], score, lowest)
+        largest = lax.fori_loop(first_pair, last_pair, score, lowest)
         largest = jnp.max(largest, axis=1, keepdims=True)
-        ones = jnp.ones((width, 128), jnp.bfloat16)
-
-        def add(c, total):
-            block = jnp.where(c == 2, VALUE_BLOCK[2], c + VALUE_BLOCK[0])
-
-            def one(pair, total):
-                weights = jnp.exp2((scores[place(c, pair), :, :width] - largest) * scale)
-                value = jnp.concatenate([pair_of(block, pair), ones], axis=1)
-                return total + jnp.dot(
-                    weights.astype(jnp.bfloat16), value, preferred_element_type=jnp.float32
-                )
-
-            return lax.fori_loop(first_pair, last_pair, one, total)
-
-        total = lax.fori_loop(columns[0], columns[1], add, jnp.zeros((2 * unit, 256), jnp.float32))
+
+        def weigh(pair, block):
+            low, high = block
+            return jnp.exp2((scores[pair - tile, :, low:high] - largest) * scale).astype(jnp.bfloat16)
+
+        def add(pair, total):
+            values = jnp.concatenate([pair_of(VALUE_BLOCK[c], pair) for c in across], axis=0)
+            weights = weigh(pair, blocks[0])
+            for index, (low, high) in enumerate(blocks):
+                current = weights
+                if index + 1 < len(blocks):
+                    weights = weigh(pair, blocks[index + 1])
+                value = jnp.concatenate([values[low:high], jnp.ones((high - low, 128), jnp.bfloat16)], axis=1)
+                total = total + jnp.dot(current, value, preferred_element_type=jnp.float32)
+            return total
+
+        total = lax.fori_loop(first_pair, last_pair, add, jnp.zeros((2 * unit, 256), jnp.float32))
         result = (total[:, :128] / total[:, 128:]).astype(o.dtype)
         for half in (0, 1):
             o[column, 2 * tile + half, at, :] = result[half * unit : (half + 1) * unit]
@@ -352,7 +351,7 @@
         scratch_shapes=[
             pltpu.VMEM((3 * columns, own + 4, piece * height, HEAD_DIM), jnp.bfloat16),
             pltpu.VMEM((columns, own, piece * height, HEAD_DIM), jnp.bfloat16),
-            pltpu.VMEM((9, 2 * unit, 6 * unit), jnp.float32),
+            pltpu.VMEM((3, 2 * unit, 18 * unit), jnp.float32),
             pltpu.SemaphoreType.DMA((len(PHASES), heads)),
             pltpu.SemaphoreType.DMA((len(PHASES), own * height)),
             pltpu.SemaphoreType.DMA((columns, own * height)),

time: 206 us -> 184 us (0.89)
  Pallas kernels: 195 us -> 173 us
    pallas_call x1, Pallas kernels: 195 us -> 173 us  [body(): pl.pallas_call(functools.partial(kernel, dims), out_shape=jax.ShapeDtypeS...]
where the time goes in v3:
time: 184 us; the launch traced here: 183 us
  Pallas kernels  173 us (94%)
  local copies, waits for them, and re-layouts  10.1 us (5%)
    pallas_call x1, Pallas kernels, body(): pl.pallas_call(functools.partial(kernel, dims), out_shape=jax.ShapeDtypeS...  173 us
    reshape x3, local copies, waits for them, and re-layouts, by_head(): value = value.reshape(frames, rows, columns, TILE_W, heads, HEAD_DIM)  4 us

profile of v3, /device:TPU:2, one launch (start us, length us, event | category | flops | bytes accessed | tf_op | source)
XLA Modules:
  0.0 183.0 jit_solution(17219559456287123496)
XLA Ops:
  0.0 0.0 copy-start.1
  0.0 1.9 %copy.6 = bf16[3,6,3,8,16,128]{5,3,0,1,2,4:T(8,128)(2,1)S(1)} copy(bf16[3,6,3,8,16,128]{5,3,4,2,1,0:T(8,128)(2,1)} %bitcast.25) | data formatting | bytes 3538944 | tf_op jit(solution)/shard_map/reshape | solution.py:338
  1.9 1.8 copy.4
  3.7 0.0 copy-done.1
  3.7 0.3 copy.5
  4.0 0.1 slice_dynamic-update-slice_fusion.2
  4.1 0.2 slice_dynamic-update-slice_fusion.1
  4.3 0.1 slice_dynamic-update-slice_fusion.5
  4.4 0.1 slice_dynamic-update-slice_fusion.4
  4.4 0.1 slice_dynamic-update-slice_fusion.3
  4.5 0.2 slice_dynamic-update-slice_fusion.x_ref
  4.7 0.0 copy-start
  4.7 2.3 %copy-done = bf16[16,9,144,128]{3,2,1,0:T(8,128)(2,1)} copy-done((bf16[16,9,144,128]{3,2,1,0:T(8,128)(2,1)}, bf16[16,9,144,128]{3,2,1,0:T(8,128)(2,1)S(1)}, u32[]{:S(2)}) %copy-start) | copy-done | bytes 5308440
  7.0 172.8 %shard_map.37 = bf16[16,3,144,128]{3,2,1,0:T(8,128)(2,1)} custom-call(bf16[16,9,144,128]{3,2,1,0:T(8,128)(2,1)} %copy-done), custom_call_target="tpu_custom_call" | custom-call | tf_op jit(solution)/shard_map/pallas_call | solution.py:346
  179.8 3.2 %copy.9 = bf16[3,6,3,8,16,128]{5,3,4,2,1,0:T(8,128)(2,1)} copy(bf16[3,6,3,8,16,128]{5,3,0,1,2,4:T(8,128)(2,1)} %bitcast.18) | data formatting | bytes 3538944 | tf_op jit(solution)/shard_map/transpose | solution.py:367
Async XLA Ops:
  0.0 3.7 %copy-start.1 = (bf16[3,6,24,2048]{3,2,1,0:T(8,128)(2,1)S(1)}, bf16[3,6,24,2048]{3,2,1,0:T(8,128)(2,1)}, u32[]{:S(2)}) copy-start(bf16[3,6,24,2048]{3,2,1,0:T(8,128)(2,1)} %param.5) | copy-start | bytes 5308420
  4.7 2.3 %copy-start = (bf16[16,9,144,128]{3,2,1,0:T(8,128)(2,1)}, bf16[16,9,144,128]{3,2,1,0:T(8,128)(2,1)S(1)}, u32[]{:S(2)}) copy-start(bf16[16,9,144,128]{3,2,1,0:T(8,128)(2,1)S(1)} %slice_dynamic-update-slice_fusion.x_ref) | copy-start | bytes 15925252

commit v4 on v3

--- a/solution.py
+++ b/solution.py
@@ -23,7 +23,7 @@
 HALO = ((0, 4), (5, 2))
 
 
-def kernel(dims, x_ref, out_ref, y, o, scores, send, recv, osend, orecv, hsend, hrecv):
+def kernel(dims, x_ref, out_ref, y, o, scores, peak, edge_keys, inner_keys, send, recv, osend, orecv, hsend, hrecv):
     heads, tm, height, frames, rows, tall = dims
     heads_here = heads // height
     group = tm // heads_here
@@ -170,6 +170,20 @@
         def _():
             halo(phase, False).wait_send()
 
+    def turn_keys(new):
+        def one(pair, carry):
+            for c in new:
+                first, second = (y[KEY_BLOCK[c], 2 * pair + half] for half in (0, 1))
+                for which, low in enumerate((0, unit)):
+                    both = jnp.concatenate([first[low : low + 2 * unit], second[low : low + 2 * unit]], axis=0)
+                    edge_keys[which, c, pair] = both.T
+                inner_keys[c, pair] = jnp.concatenate([first, second], axis=0).T
+            return carry
+
+        first_pair = jnp.where(part == 0, 1, 0)
+        last_pair = tiles + jnp.where(part == group - 1, 1, 2)
+        lax.fori_loop(first_pair, last_pair, one, 0)
+
     def attend(column, row, span, tile):
         columns = (max(column - 1, 0), min(column + 2, 3))
         first_pair = tile + jnp.where((part == 0) & (tile == 0), 1, 0)
@@ -187,12 +201,13 @@
         across = range(columns[0], columns[1])
         blocks = [(low, min(low + BLOCK, width * len(across))) for low in range(0, width * len(across), BLOCK)]
 
+        def turned(c, pair):
+            return edge_keys[lax.div(row, 2), c, pair] if span == 2 else inner_keys[c, pair]
+
         def score(pair, largest):
-            keys = jnp.concatenate([pair_of(KEY_BLOCK[c], pair) for c in across], axis=0)
+            keys = jnp.concatenate([turned(c, pair) for c in across], axis=1)
             for low, high in blocks:
-                found = lax.dot_general(
-                    query, keys[low:high], (((1,), (1,)), ((), ())), preferred_element_type=jnp.float32
-                )
+                found = jnp.dot(query, keys[:, low:high], preferred_element_type=jnp.float32)
                 scores[pair - tile, :, low:high] = found
                 for lane in range(0, high - low, 128):
                     largest = jnp.maximum(largest, found[:, lane : lane + 128])
@@ -200,11 +215,15 @@
 
         lowest = jnp.full((2 * unit, 128), -jnp.inf, jnp.float32)
         largest = lax.fori_loop(first_pair, last_pair, score, lowest)
-        largest = jnp.max(largest, axis=1, keepdims=True)
+        peak[...] = jnp.broadcast_to(jnp.max(largest, axis=1, keepdims=True), peak.shape)
 
         def weigh(pair, block):
-            low, high = block
-            return jnp.exp2((scores[pair - tile, :, low:high] - largest) * scale).astype(jnp.bfloat16)
+            top = peak[...]
+            parts = [
+                jnp.exp2((scores[pair - tile, :, lane : lane + 128] - top) * scale).astype(jnp.bfloat16)
+                for lane in range(block[0], block[1], 128)
+            ]
+            return jnp.concatenate(parts, axis=1)
 
         def add(pair, total):
             values = jnp.concatenate([pair_of(VALUE_BLOCK[c], pair) for c in across], axis=0)
@@ -316,6 +335,7 @@
         receive_phase(phase)
         if phase < len(HALO):
             exchange_halo(phase)
+            turn_keys(((0, 1), (2,))[phase])
         attend_column(phase)
     for phase in range(len(PHASES)):
         finish_sends(phase)
@@ -352,6 +372,9 @@
             pltpu.VMEM((3 * columns, own + 4, piece * height, HEAD_DIM), jnp.bfloat16),
             pltpu.VMEM((columns, own, piece * height, HEAD_DIM), jnp.bfloat16),
             pltpu.VMEM((3, 2 * unit, 18 * unit), jnp.float32),
+            pltpu.VMEM((2 * unit, 128), jnp.float32),
+            pltpu.VMEM((2, columns, own // 2 + 2, HEAD_DIM, 4 * unit), jnp.bfloat16),
+            pltpu.VMEM((columns, own // 2 + 2, HEAD_DIM, 6 * unit), jnp.bfloat16),
             pltpu.SemaphoreType.DMA((len(PHASES), heads)),
             pltpu.SemaphoreType.DMA((len(PHASES), own * height)),
             pltpu.SemaphoreType.DMA((columns, own * height)),

time: 184 us -> 185 us (level)
  no operation moved by 1% of the time
where the time goes in v4:
time: 185 us; the launch traced here: 183 us
  Pallas kernels  173 us (94%)
  local copies, waits for them, and re-layouts  10.1 us (5%)
    pallas_call x1, Pallas kernels, body(): pl.pallas_call(functools.partial(kernel, dims), out_shape=jax.ShapeDtypeS...  173 us
    reshape x3, local copies, waits for them, and re-layouts, by_head(): value = value.reshape(frames, rows, columns, TILE_W, heads, HEAD_DIM)  4 us

profile of v4, /device:TPU:2, one launch (start us, length us, event | category | flops | bytes accessed | tf_op | source)
XLA Modules:
  0.0 182.8 jit_solution(4797789130425350115)
XLA Ops:
  0.0 0.0 copy-start.1
  0.0 1.9 %copy.6 = bf16[3,6,3,8,16,128]{5,3,0,1,2,4:T(8,128)(2,1)S(1)} copy(bf16[3,6,3,8,16,128]{5,3,4,2,1,0:T(8,128)(2,1)} %bitcast.25) | data formatting | bytes 3538944 | tf_op jit(solution)/shard_map/reshape | solution.py:358
  1.9 1.8 copy.4
  3.7 0.0 copy-done.1
  3.7 0.3 copy.5
  4.0 0.1 slice_dynamic-update-slice_fusion.2
  4.1 0.2 slice_dynamic-update-slice_fusion.1
  4.3 0.1 slice_dynamic-update-slice_fusion.5
  4.4 0.1 slice_dynamic-update-slice_fusion.4
  4.4 0.1 slice_dynamic-update-slice_fusion.3
  4.5 0.2 slice_dynamic-update-slice_fusion.x_ref
  4.7 0.0 copy-start
  4.7 2.3 %copy-done = bf16[16,9,144,128]{3,2,1,0:T(8,128)(2,1)} copy-done((bf16[16,9,144,128]{3,2,1,0:T(8,128)(2,1)}, bf16[16,9,144,128]{3,2,1,0:T(8,128)(2,1)S(1)}, u32[]{:S(2)}) %copy-start) | copy-done | bytes 5308440
  7.0 172.6 %shard_map.37 = bf16[16,3,144,128]{3,2,1,0:T(8,128)(2,1)} custom-call(bf16[16,9,144,128]{3,2,1,0:T(8,128)(2,1)} %copy-done), custom_call_target="tpu_custom_call" | custom-call | tf_op jit(solution)/shard_map/pallas_call | solution.py:366
  179.7 3.2 %copy.9 = bf16[3,6,3,8,16,128]{5,3,4,2,1,0:T(8,128)(2,1)} copy(bf16[3,6,3,8,16,128]{5,3,0,1,2,4:T(8,128)(2,1)} %bitcast.18) | data formatting | bytes 3538944 | tf_op jit(solution)/shard_map/transpose | solution.py:390
Async XLA Ops:
  0.0 3.7 %copy-start.1 = (bf16[3,6,24,2048]{3,2,1,0:T(8,128)(2,1)S(1)}, bf16[3,6,24,2048]{3,2,1,0:T(8,128)(2,1)}, u32[]{:S(2)}) copy-start(bf16[3,6,24,2048]{3,2,1,0:T(8,128)(2,1)} %param.5) | copy-start | bytes 5308420
  4.7 2.3 %copy-start = (bf16[16,9,144,128]{3,2,1,0:T(8,128)(2,1)}, bf16[16,9,144,128]{3,2,1,0:T(8,128)(2,1)S(1)}, u32[]{:S(2)}) copy-start(bf16[16,9,144,128]{3,2,1,0:T(8,128)(2,1)S(1)} %slice_dynamic-update-slice_fusion.x_ref) | copy-start | bytes 15925252

commit v5 on v3

--- a/solution.py
+++ b/solution.py
@@ -1,5 +1,6 @@
 import functools
 import math
+import types
 
 import jax
 import jax.numpy as jnp
@@ -23,7 +24,7 @@
 HALO = ((0, 4), (5, 2))
 
 
-def kernel(dims, x_ref, out_ref, y, o, scores, send, recv, osend, orecv, hsend, hrecv):
+def kernel(dims, x_ref, out_ref, y, o, even, odd, send, recv, osend, orecv, hsend, hrecv):
     heads, tm, height, frames, rows, tall = dims
     heads_here = heads // height
     group = tm // heads_here
@@ -40,6 +41,8 @@
     my_slot = lax.rem(me_t, own)
     me = me_t * height + me_z
     hops = sorted(range(height), key=lambda hop: abs(hop - height / 2))
+
+    stores = (even, odd)
 
     barrier = pltpu.get_barrier_semaphore()
 
@@ -170,73 +173,91 @@
         def _():
             halo(phase, False).wait_send()
 
-    def attend(column, row, span, tile):
-        columns = (max(column - 1, 0), min(column + 2, 3))
+    def job_of(column, row, span, tile, scores):
+        across = range(max(column - 1, 0), min(column + 2, 3))
+        width = 2 * span * unit * len(across)
+        blocks = [(low, min(low + BLOCK, width)) for low in range(0, width, BLOCK)]
+        at = pl.ds(row * unit, unit)
+        near = pl.ds(max(row - 1, 0) * unit, span * unit)
+        query = jnp.concatenate(
+            [y[QUERY_BLOCK[column], 2 + 2 * tile + half, at, :] for half in (0, 1)], axis=0
+        )
+
+        def gather(table, pair):
+            return jnp.concatenate(
+                [y[table[c], 2 * pair + half, near, :] for c in across for half in (0, 1)], axis=0
+            )
+
+        def score(pair, keys, index, largest):
+            low, high = blocks[index]
+            found = lax.dot_general(
+                query, keys[low:high], (((1,), (1,)), ((), ())), preferred_element_type=jnp.float32
+            )
+            scores[pair - tile, :, low:high] = found
+            for lane in range(0, high - low, 128):
+                largest = jnp.maximum(largest, found[:, lane : lane + 128])
+            return largest
+
+        def weigh(pair, index, top):
+            low, high = blocks[index]
+            return jnp.exp2((scores[pair - tile, :, low:high] - top) * scale).astype(jnp.bfloat16)
+
+        def add(weights, values, index, total):
+            low, high = blocks[index]
+            value = jnp.concatenate([values[low:high], jnp.ones((high - low, 128), jnp.bfloat16)], axis=1)
+            return total + jnp.dot(weights, value, preferred_element_type=jnp.float32)
+
+        def finish(total):
+            result = (total[:, :128] / total[:, 128:]).astype(o.dtype)
+            for half in (0, 1):
+                o[column, 2 * tile + half, at, :] = result[half * unit : (half + 1) * unit]
+
+        return types.SimpleNamespace(
+            count=len(blocks), keys=lambda pair: gather(KEY_BLOCK, pair),
+            values=lambda pair: gather(VALUE_BLOCK, pair), score=score, weigh=weigh, add=add, finish=finish,
+        )
+
+    def attend(column, tile):
         first_pair = tile + jnp.where((part == 0) & (tile == 0), 1, 0)
         last_pair = tile + jnp.where((part == group - 1) & (tile == tiles - 1), 2, 3)
-        width = 2 * span * unit
-        at = pl.ds(pl.multiple_of(row * unit, unit), unit)
-        near = pl.ds(pl.multiple_of(jnp.maximum(row - 1, 0) * unit, unit), span * unit)
-        query = jnp.concatenate(
-            [y[QUERY_BLOCK[column], 2 + 2 * tile + half, at, :] for half in (0, 1)], axis=0
-        )
-
-        def pair_of(block, pair):
-            return jnp.concatenate([y[block, 2 * pair + half, near, :] for half in (0, 1)], axis=0)
-
-        across = range(columns[0], columns[1])
-        blocks = [(low, min(low + BLOCK, width * len(across))) for low in range(0, width * len(across), BLOCK)]
-
-        def score(pair, largest):
-            keys = jnp.concatenate([pair_of(KEY_BLOCK[c], pair) for c in across], axis=0)
-            for low, high in blocks:
-                found = lax.dot_general(
-                    query, keys[low:high], (((1,), (1,)), ((), ())), preferred_element_type=jnp.float32
-                )
-                scores[pair - tile, :, low:high] = found
-                for lane in range(0, high - low, 128):
-                    largest = jnp.maximum(largest, found[:, lane : lane + 128])
-            return largest
-
-        lowest = jnp.full((2 * unit, 128), -jnp.inf, jnp.float32)
-        largest = lax.fori_loop(first_pair, last_pair, score, lowest)
-        largest = jnp.max(largest, axis=1, keepdims=True)
-
-        def weigh(pair, block):
-            low, high = block
-            return jnp.exp2((scores[pair - tile, :, low:high] - largest) * scale).astype(jnp.bfloat16)
-
-        def add(pair, total):
-            values = jnp.concatenate([pair_of(VALUE_BLOCK[c], pair) for c in across], axis=0)
-            weights = weigh(pair, blocks[0])
-            for index, (low, high) in enumerate(blocks):
-                current = weights
-                if index + 1 < len(blocks):
-                    weights = weigh(pair, blocks[index + 1])
-                value = jnp.concatenate([values[low:high], jnp.ones((high - low, 128), jnp.bfloat16)], axis=1)
-                total = total + jnp.dot(current, value, preferred_element_type=jnp.float32)
-            return total
-
-        total = lax.fori_loop(first_pair, last_pair, add, jnp.zeros((2 * unit, 256), jnp.float32))
-        result = (total[:, :128] / total[:, 128:]).astype(o.dtype)
-        for half in (0, 1):
-            o[column, 2 * tile + half, at, :] = result[half * unit : (half + 1) * unit]
+        row_tiles = tall // TILE_H
+        order = [(0, 2), (row_tiles - 1, 2)] + [(row, 3) for row in range(1, row_tiles - 1)]
+        adding, top = None, None
+        for index in range(len(order) + 1):
+            scoring = None
+            if index < len(order):
+                scoring = job_of(column, *order[index], tile, stores[index % 2])
+
+            def step(pair, carry, adding=adding, scoring=scoring, top=top):
+                total, largest = carry
+                if adding:
+                    values = adding.values(pair)
+                    weights = adding.weigh(pair, 0, top)
+                if scoring:
+                    keys = scoring.keys(pair)
+                for block in range(max(job.count for job in (adding, scoring) if job)):
+                    if scoring and block < scoring.count:
+                        largest = scoring.score(pair, keys, block, largest)
+                    if adding and block < adding.count:
+                        current = weights
+                        if block + 1 < adding.count:
+                            weights = adding.weigh(pair, block + 1, top)
+                        total = adding.add(current, values, block, total)
+                return total, largest
+
+            total = jnp.zeros((2 * unit, 256), jnp.float32) if adding else None
+            largest = jnp.full((2 * unit, 128), -jnp.inf, jnp.float32) if scoring else None
+            total, largest = lax.fori_loop(first_pair, last_pair, step, (total, largest))
+            if adding:
+                adding.finish(total)
+            if scoring:
+                top = jnp.max(largest, axis=1, keepdims=True)
+            adding = scoring
 
     def attend_column(column):
         def one(step, carry):
             tile = jnp.where(lax.rem(part, 2) == 0, step, tiles - 1 - step)
-            row_tiles = tall // TILE_H
-
-            def edge(which, carry):
-                attend(column, which * (row_tiles - 1), 2, tile)
-                return carry
-
-            def inner(row, carry):
-                attend(column, row, 3, tile)
-                return carry
-
-            lax.fori_loop(0, 2, edge, 0)
-            lax.fori_loop(1, row_tiles - 1, inner, 0)
+            attend(column, tile)
             return_tile(column, tile)
             return carry
 
@@ -352,6 +373,7 @@
             pltpu.VMEM((3 * columns, own + 4, piece * height, HEAD_DIM), jnp.bfloat16),
             pltpu.VMEM((columns, own, piece * height, HEAD_DIM), jnp.bfloat16),
             pltpu.VMEM((3, 2 * unit, 18 * unit), jnp.float32),
+            pltpu.VMEM((3, 2 * unit, (12 if tall == 3 * TILE_H else 18) * unit), jnp.float32),
             pltpu.SemaphoreType.DMA((len(PHASES), heads)),
             pltpu.SemaphoreType.DMA((len(PHASES), own * height)),
             pltpu.SemaphoreType.DMA((columns, own * height)),

time: 184 us -> 181 us (0.984)
  Pallas kernels: 173 us -> 170 us
    pallas_call x1, Pallas kernels: 173 us -> 170 us  [body(): pl.pallas_call(functools.partial(kernel, dims), out_shape=jax.ShapeDtypeS...]
where the time goes in v5:
time: 181 us; the launch traced here: 180 us
  Pallas kernels  170 us (94%)
  local copies, waits for them, and re-layouts  10.1 us (6%)
    pallas_call x1, Pallas kernels, body(): pl.pallas_call(functools.partial(kernel, dims), out_shape=jax.ShapeDtypeS...  170 us
    reshape x3, local copies, waits for them, and re-layouts, by_head(): value = value.reshape(frames, rows, columns, TILE_W, heads, HEAD_DIM)  4 us

profile of v5, /device:TPU:2, one launch (start us, length us, event | category | flops | bytes accessed | tf_op | source)
XLA Modules:
  0.0 180.0 jit_solution(5796521832591768182)
XLA Ops:
  0.0 0.0 copy-start.1
  0.0 1.9 %copy.6 = bf16[3,6,3,8,16,128]{5,3,0,1,2,4:T(8,128)(2,1)S(1)} copy(bf16[3,6,3,8,16,128]{5,3,4,2,1,0:T(8,128)(2,1)} %bitcast.25) | data formatting | bytes 3538944 | tf_op jit(solution)/shard_map/reshape | solution.py:359
  1.9 1.8 copy.4
  3.7 0.0 copy-done.1
  3.7 0.3 copy.5
  4.0 0.1 slice_dynamic-update-slice_fusion.2
  4.1 0.2 slice_dynamic-update-slice_fusion.1
  4.3 0.1 slice_dynamic-update-slice_fusion.5
  4.4 0.1 slice_dynamic-update-slice_fusion.4
  4.4 0.1 slice_dynamic-update-slice_fusion.3
  4.5 0.2 slice_dynamic-update-slice_fusion.x_ref
  4.7 0.0 copy-start
  4.7 2.3 %copy-done = bf16[16,9,144,128]{3,2,1,0:T(8,128)(2,1)} copy-done((bf16[16,9,144,128]{3,2,1,0:T(8,128)(2,1)}, bf16[16,9,144,128]{3,2,1,0:T(8,128)(2,1)S(1)}, u32[]{:S(2)}) %copy-start) | copy-done | bytes 5308440
  7.0 169.8 %shard_map.37 = bf16[16,3,144,128]{3,2,1,0:T(8,128)(2,1)} custom-call(bf16[16,9,144,128]{3,2,1,0:T(8,128)(2,1)} %copy-done), custom_call_target="tpu_custom_call" | custom-call | tf_op jit(solution)/shard_map/pallas_call | solution.py:367
  176.8 3.2 %copy.9 = bf16[3,6,3,8,16,128]{5,3,4,2,1,0:T(8,128)(2,1)} copy(bf16[3,6,3,8,16,128]{5,3,0,1,2,4:T(8,128)(2,1)} %bitcast.18) | data formatting | bytes 3538944 | tf_op jit(solution)/shard_map/transpose | solution.py:389
Async XLA Ops:
  0.0 3.7 %copy-start.1 = (bf16[3,6,24,2048]{3,2,1,0:T(8,128)(2,1)S(1)}, bf16[3,6,24,2048]{3,2,1,0:T(8,128)(2,1)}, u32[]{:S(2)}) copy-start(bf16[3,6,24,2048]{3,2,1,0:T(8,128)(2,1)} %param.5) | copy-start | bytes 5308420
  4.7 2.3 %copy-start = (bf16[16,9,144,128]{3,2,1,0:T(8,128)(2,1)}, bf16[16,9,144,128]{3,2,1,0:T(8,128)(2,1)S(1)}, u32[]{:S(2)}) copy-start(bf16[16,9,144,128]{3,2,1,0:T(8,128)(2,1)S(1)} %slice_dynamic-update-slice_fusion.x_ref) | copy-start | bytes 15925252

commit v6 on v5

--- a/solution.py
+++ b/solution.py
@@ -258,7 +258,8 @@
         def one(step, carry):
             tile = jnp.where(lax.rem(part, 2) == 0, step, tiles - 1 - step)
             attend(column, tile)
-            return_tile(column, tile)
+            if column > 0:
+                return_tile(column, tile)
             return carry
 
         lax.fori_loop(0, tiles, one, 0)
@@ -331,15 +332,22 @@
 
         lax.fori_loop(0, heads, landed, 0)
 
-    for phase in range(len(PHASES)):
-        start_phase(phase)
-    for phase in range(len(PHASES)):
-        receive_phase(phase)
-        if phase < len(HALO):
-            exchange_halo(phase)
-        attend_column(phase)
-    for phase in range(len(PHASES)):
-        finish_sends(phase)
+    start_phase(0)
+    finish_sends(0)
+    start_phase(1)
+    receive_phase(0)
+    exchange_halo(0)
+    attend_column(0)
+    receive_phase(1)
+    start_phase(2)
+    for tile in range(tiles):
+        return_tile(0, tile)
+    exchange_halo(1)
+    attend_column(1)
+    receive_phase(2)
+    attend_column(2)
+    finish_sends(1)
+    finish_sends(2)
     for phase in range(len(HALO)):
         finish_halo(phase)
     for column in (0, 1, 2):
@@ -382,7 +390,7 @@
             pltpu.SemaphoreType.DMA((2, 2)),
         ],
         compiler_params=pltpu.CompilerParams(
-            collective_id=0, has_side_effects=True, vmem_limit_bytes=56 * 1024 * 1024
+            collective_id=0, has_side_effects=True, vmem_limit_bytes=48 * 1024 * 1024
         ),
     )(blocks)
     result = result.reshape(heads, columns, rows, frames, TILE_W, HEAD_DIM)

time: 181 us -> 171 us (0.945)
  Pallas kernels: 170 us -> 161 us
    pallas_call x1, Pallas kernels: 170 us -> 161 us  [body(): pl.pallas_call(functools.partial(kernel, dims), out_shape=jax.ShapeDtypeS...]
where the time goes in v6:
time: 171 us; the launch traced here: 170 us
  Pallas kernels  161 us (94%)
  local copies, waits for them, and re-layouts  8.64 us (5%)
    pallas_call x1, Pallas kernels, body(): pl.pallas_call(functools.partial(kernel, dims), out_shape=jax.ShapeDtypeS...  161 us
    reshape x3, local copies, waits for them, and re-layouts, by_head(): value = value.reshape(frames, rows, columns, TILE_W, heads, HEAD_DIM)  4 us

profile of v6, /device:TPU:2, one launch (start us, length us, event | category | flops | bytes accessed | tf_op | source)
XLA Modules:
  0.0 170.0 jit_solution(12481660584837302039)
XLA Ops:
  0.0 0.0 copy-start.1
  0.0 1.9 %copy.6 = bf16[3,6,3,8,16,128]{5,3,0,1,2,4:T(8,128)(2,1)S(1)} copy(bf16[3,6,3,8,16,128]{5,3,4,2,1,0:T(8,128)(2,1)} %bitcast.25) | data formatting | bytes 3538944 | tf_op jit(solution)/shard_map/reshape | solution.py:367
  1.9 1.8 %copy.4 = bf16[3,6,3,8,16,128]{5,3,0,1,2,4:T(8,128)(2,1)S(1)} copy(bf16[3,6,3,8,16,128]{5,3,4,2,1,0:T(8,128)(2,1)} %bitcast.26) | data formatting | bytes 3538944 | tf_op jit(solution)/shard_map/reshape | solution.py:367
  3.7 0.0 copy-done.1
  3.7 0.3 copy.5
  4.0 0.1 slice_dynamic-update-slice_fusion.2
  4.1 0.2 slice_dynamic-update-slice_fusion.1
  4.3 0.1 slice_dynamic-update-slice_fusion.5
  4.4 0.1 slice_dynamic-update-slice_fusion.4
  4.4 0.1 slice_dynamic-update-slice_fusion.3
  4.5 0.2 slice_dynamic-update-slice_fusion.x_ref
  4.7 0.0 copy-start
  4.7 2.3 %copy-done = bf16[16,9,144,128]{3,2,1,0:T(8,128)(2,1)} copy-done((bf16[16,9,144,128]{3,2,1,0:T(8,128)(2,1)}, bf16[16,9,144,128]{3,2,1,0:T(8,128)(2,1)S(1)}, u32[]{:S(2)}) %copy-start) | copy-done | bytes 5308440
  7.0 161.3 %shard_map.37 = bf16[16,3,144,128]{3,2,1,0:T(8,128)(2,1)S(1)} custom-call(bf16[16,9,144,128]{3,2,1,0:T(8,128)(2,1)} %copy-done), custom_call_target="tpu_custom_call" | custom-call | tf_op jit(solution)/shard_map/pallas_call | solution.py:375
  168.3 1.7 %copy.9 = bf16[3,6,3,8,16,128]{5,3,4,2,1,0:T(8,128)(2,1)} copy(bf16[3,6,3,8,16,128]{5,3,0,1,2,4:T(8,128)(2,1)S(1)} %bitcast.18) | data formatting | bytes 3538944 | tf_op jit(solution)/shard_map/transpose | solution.py:397
Async XLA Ops:
  0.0 3.7 %copy-start.1 = (bf16[3,6,24,2048]{3,2,1,0:T(8,128)(2,1)S(1)}, bf16[3,6,24,2048]{3,2,1,0:T(8,128)(2,1)}, u32[]{:S(2)}) copy-start(bf16[3,6,24,2048]{3,2,1,0:T(8,128)(2,1)} %param.5) | copy-start | bytes 5308420
  4.7 2.3 %copy-start = (bf16[16,9,144,128]{3,2,1,0:T(8,128)(2,1)}, bf16[16,9,144,128]{3,2,1,0:T(8,128)(2,1)S(1)}, u32[]{:S(2)}) copy-start(bf16[16,9,144,128]{3,2,1,0:T(8,128)(2,1)S(1)} %slice_dynamic-update-slice_fusion.x_ref) | copy-start | bytes 15925252
